TPU v7x, 32 devices: a whole 2x2x4 slice. The times are simulated.
32 devices in a mesh: lon: 8 (over y, x, core), lat: 4 (over z).
Axes of the slice: x: 2, y: 2, z: 4, core: 2. Of those that a mesh axis runs over, the one named last changes fastest.
Arguments:
- tracers: bfloat16 [12, 64, 32, 1024], P(None, None, 'lat', 'lon'), may hold values from 0.099609375 to 2
- east_wind: bfloat16 [64, 32, 1024], P(None, 'lat', 'lon'), may hold values from -0.44921875 to 0.44921875
- north_wind: bfloat16 [64, 32, 1024], P(None, 'lat', 'lon'), may hold values from -0.44921875 to 0.44921875
- sunlit: int32 [32, 1024], P('lat', 'lon'), may hold values from 0 to 1, as said below
- coupling: float32 [12, 12], replicated, may hold values from -0.15 to 0.15
- rate_table: float32 [8, 64], replicated, may hold values from 0.01 to 0.6
- rate_index: int32 [12], replicated, may hold values from 0 to 7
- kappa: float32 [63], replicated, may hold values from 0.05 to 0.24
Outputs:
- updated: bfloat16 [12, 64, 32, 1024], P(None, None, 'lat', 'lon')
Inputs may be any that keep to these rules, and one draw needn't show every extreme that they name: A device's block of columns holds at most 768 sunlit columns, and together with the block of the device half the lon axis away (same lat index) at most 1024; both bounds are reached in every draw.
All inputs are finite; a program needn't handle non-finite values.
Results may differ from a plain program's by a relative error of at most 0.001.
Values may be sent and summed in bfloat16 or wider, within the bound.
A program may use at most 128 MiB of HBM per device.

v0:
```python
import jax
import jax.numpy as jnp
from jax import lax
from jax.experimental import pallas as pl
from jax.experimental.pallas import tpu as pltpu
from jax.sharding import PartitionSpec as P

SUBSTEPS = 16
CHUNK = 8
F32 = jnp.float32
BF16 = jnp.bfloat16
MESH = pl.DeviceIdType.MESH


def rims_kernel(
    lon_count,
    lat_count,
    c_ref,
    u_ref,
    v_ref,
    west_ref,
    east_ref,
    south_ref,
    north_ref,
    wide,
    to_east,
    to_west,
    to_north,
    to_south,
    send_sem,
    recv_sem,
):
    species, levels, rows, cols = c_ref.shape
    lon, lat = lax.axis_index("lon"), lax.axis_index("lat")
    east, west = lax.rem(lon + 1, lon_count), lax.rem(lon + lon_count - 1, lon_count)
    has_south, has_north = lat > 0, lat < lat_count - 1

    barrier = pltpu.get_barrier_semaphore()
    for side in (east, west):
        pl.semaphore_signal(barrier, inc=1, device_id=(side, lat), device_id_type=MESH)

    @pl.when(has_south)
    def _():
        pl.semaphore_signal(barrier, inc=1, device_id=(lon, lat - 1), device_id_type=MESH)

    @pl.when(has_north)
    def _():
        pl.semaphore_signal(barrier, inc=1, device_id=(lon, lat + 1), device_id_type=MESH)

    def widen(s, _):
        wide[pl.ds(s * levels, levels)] = c_ref[s].astype(F32)
        return 0

    lax.fori_loop(0, species, widen, 0)
    wide[pl.ds(species * levels, levels)] = v_ref[...].astype(F32)
    to_south[...] = wide[:, 0, :].astype(BF16)
    to_north[...] = wide[: species * levels, rows - 1, :].astype(BF16)

    peers = 2 + jnp.where(has_south, 1, 0) + jnp.where(has_north, 1, 0)
    pl.semaphore_wait(barrier, peers)

    send_south = pltpu.make_async_remote_copy(
        src_ref=to_south,
        dst_ref=north_ref,
        send_sem=send_sem.at[0],
        recv_sem=recv_sem.at[0],
        device_id=(lon, lat - 1),
        device_id_type=MESH,
    )
    send_north = pltpu.make_async_remote_copy(
        src_ref=to_north,
        dst_ref=south_ref,
        send_sem=send_sem.at[1],
        recv_sem=recv_sem.at[1],
        device_id=(lon, lat + 1),
        device_id_type=MESH,
    )

    @pl.when(has_south)
    def _():
        send_south.start()

    @pl.when(has_north)
    def _():
        send_north.start()

    lane = lax.broadcasted_iota(jnp.int32, (rows, cols), 1)
    wide[pl.ds(species * levels, levels)] = u_ref[...].astype(F32)

    def pack(s, _):
        last = jnp.zeros((rows, cols), F32)
        first = jnp.zeros((rows, cols), F32)
        for k in range(levels):
            turned = pltpu.roll(wide[s * levels + k], (k + 1) % cols, 1)
            last = jnp.where(lane == k, turned, last)
            first = jnp.where(lane == k + 1, turned, first)
        to_east[s] = last
        to_west[s] = first
        return 0

    lax.fori_loop(0, species + 1, pack, 0)
    send_east = pltpu.make_async_remote_copy(
        src_ref=to_east,
        dst_ref=west_ref,
        send_sem=send_sem.at[2],
        recv_sem=recv_sem.at[2],
        device_id=(east, lat),
        device_id_type=MESH,
    )
    send_west = pltpu.make_async_remote_copy(
        src_ref=to_west,
        dst_ref=east_ref,
        send_sem=send_sem.at[3],
        recv_sem=recv_sem.at[3],
        device_id=(west, lat),
        device_id_type=MESH,
    )
    send_east.start()
    send_west.start()

    @pl.when(jnp.logical_not(has_south))
    def _():
        south_ref[...] = jnp.zeros_like(south_ref)

    @pl.when(jnp.logical_not(has_north))
    def _():
        north_ref[...] = jnp.zeros_like(north_ref)

    send_east.wait()
    send_west.wait()

    @pl.when(has_south)
    def _():
        send_south.wait_send()
        send_north.wait_recv()

    @pl.when(has_north)
    def _():
        send_north.wait_send()
        send_south.wait_recv()


def column_kernel(
    coupling_ref,
    table_ref,
    index_ref,
    kappa_ref,
    c_ref,
    u_ref,
    v_ref,
    light_ref,
    west_ref,
    east_ref,
    south_ref,
    north_ref,
    out_ref,
    state,
    loss,
    base,
    matrix_wide,
    matrix,
    south,
    north,
):
    species, levels, rows, cols = c_ref.shape
    mix = species * rows
    pairs = levels // 2
    lane = lax.broadcasted_iota(jnp.int32, (rows, cols), 1)
    sub = lax.broadcasted_iota(jnp.int32, (rows, cols), 0)

    col = lax.broadcasted_iota(jnp.int32, (rows, 4 * mix), 1)
    row = lax.broadcasted_iota(jnp.int32, (rows, 4 * mix), 0)
    place = lax.rem(col, mix)
    for s in range(species):
        value = jnp.zeros((rows, 4 * mix), F32)
        for t in range(species):
            entry = coupling_ref[s, t] + (1.0 if s == t else 0.0)
            value = jnp.where(place == row + t * rows, entry, value)
        high = value.astype(BF16).astype(F32)
        matrix_wide[s * rows : (s + 1) * rows, :] = jnp.where(
            col < 2 * mix, high, value - high
        )
    matrix[...] = matrix_wide[...].astype(BF16)
    south[...] = south_ref[...].astype(F32)
    north[...] = north_ref[...].astype(F32)
    at_wall = jnp.logical_and(lax.axis_index("lat") == 0, sub == 0)

    def advect(p, _):
        for half in range(2):
            k = 2 * p + half
            lanes = slice(half * cols, (half + 1) * cols)
            u = u_ref[k].astype(F32)
            v = jnp.where(at_wall, 0.0, v_ref[k].astype(F32))
            to_first = lax.rem(cols - k, cols)
            to_last = cols - 2 - k
            u_east = jnp.where(
                lane == cols - 1,
                pltpu.roll(east_ref[species], to_last, 1),
                pltpu.roll(u, cols - 1, 1),
            )
            v_north = jnp.where(
                sub == rows - 1,
                north[pl.ds(species * levels + k, 1), :],
                pltpu.roll(v, rows - 1, 0),
            )
            from_west, to_west = jnp.maximum(u, 0.0), jnp.minimum(u, 0.0)
            to_east, from_east = jnp.maximum(u_east, 0.0), jnp.minimum(u_east, 0.0)
            from_south, to_south = jnp.maximum(v, 0.0), jnp.minimum(v, 0.0)
            to_north, from_north = jnp.maximum(v_north, 0.0), jnp.minimum(v_north, 0.0)
            stay = 1.0 - (to_east - to_west) - (to_north - to_south)
            for s in range(species):
                c = c_ref[s, k].astype(F32)
                c_west = jnp.where(
                    lane == 0, pltpu.roll(west_ref[s], to_first, 1), pltpu.roll(c, 1, 1)
                )
                c_east = jnp.where(
                    lane == cols - 1,
                    pltpu.roll(east_ref[s], to_last, 1),
                    pltpu.roll(c, cols - 1, 1),
                )
                c_south = jnp.where(
                    sub == 0, south[pl.ds(s * levels + k, 1), :], pltpu.roll(c, 1, 0)
                )
                c_north = jnp.where(
                    sub == rows - 1,
                    north[pl.ds(s * levels + k, 1), :],
                    pltpu.roll(c, rows - 1, 0),
                )
                value = (
                    stay * c
                    + (from_west * c_west - from_east * c_east)
                    + (from_south * c_south - from_north * c_north)
                ).astype(BF16)
                out_ref[s, k] = value
                tile = slice(s * rows, (s + 1) * rows)
                state[p + 1, tile, lanes] = value.astype(F32)
                rate = table_ref[index_ref[s], k]
                loss[p, tile, lanes] = jnp.full((rows, cols), rate, F32)
                base[p, tile, lanes] = jnp.full((rows, cols), 1.0 + rate, F32)
        return 0

    lax.fori_loop(0, pairs, advect, 0)

    def substep(step, _):
        def chunk(b, carry):
            below, flux = carry
            for i in range(CHUNK):
                p = b * CHUNK + i
                q = state[p + 1]
                high = q.astype(BF16)
                low = (q - high.astype(F32)).astype(BF16)
                made = jnp.dot(
                    matrix[...],
                    jnp.concatenate([high, low, high, low], axis=0),
                    preferred_element_type=F32,
                )
                under = base[p] + loss[p] * (q * q)
                guess = pl.reciprocal(under, approx=True)
                z = (made * guess) * (2.0 - under * guess)
                for half in range(2):
                    here = z[:, half * cols : (half + 1) * cols]
                    k = 2 * p + half
                    rate = jnp.where(k > 0, kappa_ref[jnp.maximum(k - 1, 0)], 0.0)
                    upward = rate * (here - below)
                    lanes = slice((1 - half) * cols, (2 - half) * cols)
                    state[p + half, :, lanes] = below + (upward - flux)
                    below, flux = here, upward
            return below, flux

        zero = jnp.zeros((mix, cols), F32)
        below, flux = lax.fori_loop(0, pairs // CHUNK, chunk, (zero, zero))
        state[pairs, :, cols:] = below - flux
        return 0

    lax.fori_loop(0, SUBSTEPS, substep, 0)

    lit = light_ref[...] > 0

    def finish(p, _):
        for half in range(2):
            k = 2 * p + half
            lanes = slice(half * cols, (half + 1) * cols)
            for s in range(species):
                done = state[p + 1, s * rows : (s + 1) * rows, lanes]
                out_ref[s, k] = jnp.where(lit, done, out_ref[s, k].astype(F32)).astype(BF16)
        return 0

    lax.fori_loop(0, pairs, finish, 0)


def vmem():
    return pl.BlockSpec(memory_space=pltpu.VMEM)


def smem():
    return pl.BlockSpec(memory_space=pltpu.SMEM)


def solution(mesh):
    placed = (
        P(None, None, "lat", "lon"),
        P(None, "lat", "lon"),
        P(None, "lat", "lon"),
        P("lat", "lon"),
        P(),
        P(),
        P(),
        P(),
    )
    lon_count, lat_count = mesh.shape["lon"], mesh.shape["lat"]

    def local(tracers, east_wind, north_wind, sunlit, coupling, rate_table, rate_index, kappa):
        species, levels, rows, cols = tracers.shape
        mix = species * rows
        pairs = levels // 2

        def rims(*refs):
            return rims_kernel(lon_count, lat_count, *refs)

        sides = pl.pallas_call(
            rims,
            out_shape=(
                jax.ShapeDtypeStruct((species + 1, rows, cols), F32),
                jax.ShapeDtypeStruct((species + 1, rows, cols), F32),
                jax.ShapeDtypeStruct((species * levels, cols), BF16),
                jax.ShapeDtypeStruct(((species + 1) * levels, cols), BF16),
            ),
            in_specs=[vmem()] * 3,
            out_specs=(vmem(),) * 4,
            scratch_shapes=[
                pltpu.VMEM(((species + 1) * levels, rows, cols), F32),
                pltpu.VMEM((species + 1, rows, cols), F32),
                pltpu.VMEM((species + 1, rows, cols), F32),
                pltpu.VMEM((species * levels, cols), BF16),
                pltpu.VMEM(((species + 1) * levels, cols), BF16),
                pltpu.SemaphoreType.DMA((4,)),
                pltpu.SemaphoreType.DMA((4,)),
            ],
            compiler_params=pltpu.CompilerParams(
                collective_id=0, has_side_effects=True, vmem_limit_bytes=32 * 2**20
            ),
            name="rims",
        )(tracers, east_wind, north_wind)
        return pl.pallas_call(
            column_kernel,
            out_shape=jax.ShapeDtypeStruct(tracers.shape, BF16),
            in_specs=[smem()] * 4 + [vmem()] * 8,
            out_specs=vmem(),
            scratch_shapes=[
                pltpu.VMEM((pairs + 1, mix, 2 * cols), F32),
                pltpu.VMEM((pairs, mix, 2 * cols), F32),
                pltpu.VMEM((pairs, mix, 2 * cols), F32),
                pltpu.VMEM((mix, 4 * mix), F32),
                pltpu.VMEM((mix, 4 * mix), BF16),
                pltpu.VMEM((species * levels, cols), F32),
                pltpu.VMEM(((species + 1) * levels, cols), F32),
            ],
            compiler_params=pltpu.CompilerParams(vmem_limit_bytes=40 * 2**20),
            name="columns",
        )(
            coupling,
            rate_table,
            rate_index,
            kappa,
            tracers,
            east_wind,
            north_wind,
            sunlit,
            *sides,
        )

    return jax.shard_map(
        local, mesh=mesh, in_specs=placed, out_specs=P(None, None, "lat", "lon"), check_vma=False
    )
```

profile of v0, /device:TPU:0, one launch (start us, length us, event | category | flops | bytes accessed | tf_op | source)
XLA Modules:
  0.0 58.7 jit_solution(18408042949496375178)
XLA Ops:
  0.0 0.0 copy-start
  0.0 1.4 %copy-done = bf16[12,64,8,128]{3,2,1,0:T(8,128)(2,1)S(1)} copy-done((bf16[12,64,8,128]{3,2,1,0:T(8,128)(2,1)S(1)}, bf16[12,64,8,128]{3,2,1,0:T(8,128)(2,1)}, u32[]{:S(2)}) %copy-start) | copy-done | bytes 1572888
  1.4 0.0 copy-start.2
  1.4 0.9 %copy-done.2 = bf16[64,8,128]{2,1,0:T(8,128)(2,1)S(1)} copy-done((bf16[64,8,128]{2,1,0:T(8,128)(2,1)S(1)}, bf16[64,8,128]{2,1,0:T(8,128)(2,1)}, u32[]{:S(2)}) %copy-start.2) | copy-done | bytes 131096
  2.3 0.0 copy-start.4
  2.3 0.9 %copy-done.4 = bf16[64,8,128]{2,1,0:T(8,128)(2,1)S(1)} copy-done((bf16[64,8,128]{2,1,0:T(8,128)(2,1)S(1)}, bf16[64,8,128]{2,1,0:T(8,128)(2,1)}, u32[]{:S(2)}) %copy-start.4) | copy-done | bytes 131096
  3.2 0.0 copy-start.1
  3.2 0.0 copy-start.3
  3.2 0.0 copy-start.5
  3.2 0.0 copy-start.7
  3.2 0.0 copy-start.9
  3.2 0.0 copy-start.10
  3.2 10.2 %rims.1 = (f32[13,8,128]{2,1,0:T(8,128)S(1)}, f32[13,8,128]{2,1,0:T(8,128)S(1)}, bf16[768,128]{1,0:T(8,128)(2,1)S(1)}, bf16[832,128]{1,0:T(8,128)(2,1)S(1)}) custom-call(bf16[12,64,8,128]{3,2,1,0:T(8,128)(2,1)S(1)} %copy-done, bf16[64,8,128]{2,1,0:T(8,128)(2,1)S(1)} %copy-done.2, bf16[64,8,128]{2,1,0:T(8,128)(2,1)S(1)} %copy-done.4), custom_call_target="tpu_custom_call" | custom-call | tf_op jit(solution)/shard_map/rims/pallas_call | solution.py:320
  13.4 0.0 copy-done.1
  13.4 0.0 copy-done.3
  13.4 0.0 copy-done.5
  13.4 0.0 copy-done.7
  13.5 0.0 copy-done.9
  13.5 0.0 copy-done.10
  13.5 0.0 copy-start.6
  13.5 0.7 %copy-done.6 = f32[12,12]{1,0:T(8,128)S(1)} copy-done((f32[12,12]{1,0:T(8,128)S(1)}, f32[12,12]{1,0:T(8,128)}, u32[]{:S(2)}) %copy-start.6) | copy-done | bytes 600
  14.2 0.0 copy-start.8
  14.2 0.7 %copy-done.8 = s32[8,128]{1,0:T(8,128)S(1)} copy-done((s32[8,128]{1,0:T(8,128)S(1)}, s32[8,128]{1,0:T(8,128)}, u32[]{:S(2)}) %copy-start.8) | copy-done | bytes 4120
  14.9 43.9 %columns.1 = bf16[12,64,8,128]{3,2,1,0:T(8,128)(2,1)} custom-call(f32[12,12]{1,0:T(8,128)S(1)} %copy-done.6, f32[8,64]{1,0:T(8,128)S(1)} %copy-done.7, s32[12]{0:T(128)S(1)} %copy-done.9, f32[63]{0:T(128)S(1)} %copy-done.10, bf16[12,64,8,128]{3,2,1,0:T(8,128)(2,1)S(1)} %copy-done.1, bf16[64,8,128]{2,1,0:T(8,128)(2,1)S(1)} %copy-done.3, ...), custom_call_target="tpu_custom_call" | custom-call | tf_op jit(solution)/shard_map/columns/pallas_call | solution.py:344
Async XLA Ops:
  0.0 1.4 %copy-start = (bf16[12,64,8,128]{3,2,1,0:T(8,128)(2,1)S(1)}, bf16[12,64,8,128]{3,2,1,0:T(8,128)(2,1)}, u32[]{:S(2)}) copy-start(bf16[12,64,8,128]{3,2,1,0:T(8,128)(2,1)} %c_ref.1) | copy-start | bytes 4718596
  1.4 0.9 %copy-start.2 = (bf16[64,8,128]{2,1,0:T(8,128)(2,1)S(1)}, bf16[64,8,128]{2,1,0:T(8,128)(2,1)}, u32[]{:S(2)}) copy-start(bf16[64,8,128]{2,1,0:T(8,128)(2,1)} %u_ref.1) | copy-start | bytes 393220
  2.3 0.9 %copy-start.4 = (bf16[64,8,128]{2,1,0:T(8,128)(2,1)S(1)}, bf16[64,8,128]{2,1,0:T(8,128)(2,1)}, u32[]{:S(2)}) copy-start(bf16[64,8,128]{2,1,0:T(8,128)(2,1)} %v_ref.1) | copy-start | bytes 393220
  3.2 10.2 %copy-start.1 = (bf16[12,64,8,128]{3,2,1,0:T(8,128)(2,1)S(1)}, bf16[12,64,8,128]{3,2,1,0:T(8,128)(2,1)}, u32[]{:S(2)}) copy-start(bf16[12,64,8,128]{3,2,1,0:T(8,128)(2,1)} %c_ref.1) | copy-start | bytes 4718596
  3.2 10.2 %copy-start.3 = (bf16[64,8,128]{2,1,0:T(8,128)(2,1)S(1)}, bf16[64,8,128]{2,1,0:T(8,128)(2,1)}, u32[]{:S(2)}) copy-start(bf16[64,8,128]{2,1,0:T(8,128)(2,1)} %u_ref.1) | copy-start | bytes 393220
  3.2 10.2 %copy-start.5 = (bf16[64,8,128]{2,1,0:T(8,128)(2,1)S(1)}, bf16[64,8,128]{2,1,0:T(8,128)(2,1)}, u32[]{:S(2)}) copy-start(bf16[64,8,128]{2,1,0:T(8,128)(2,1)} %v_ref.1) | copy-start | bytes 393220
  3.2 10.2 %copy-start.7 = (f32[8,64]{1,0:T(8,128)S(1)}, f32[8,64]{1,0:T(8,128)}, u32[]{:S(2)}) copy-start(f32[8,64]{1,0:T(8,128)} %table_ref.1) | copy-start | bytes 6148
  3.2 10.2 %copy-start.9 = (s32[12]{0:T(128)S(1)}, s32[12]{0:T(128)}, u32[]{:S(2)}) copy-start(s32[12]{0:T(128)} %index_ref.1) | copy-start | bytes 148
  3.2 10.2 %copy-start.10 = (f32[63]{0:T(128)S(1)}, f32[63]{0:T(128)}, u32[]{:S(2)}) copy-start(f32[63]{0:T(128)} %kappa_ref.1) | copy-start | bytes 760
  13.5 0.7 %copy-start.6 = (f32[12,12]{1,0:T(8,128)S(1)}, f32[12,12]{1,0:T(8,128)}, u32[]{:S(2)}) copy-start(f32[12,12]{1,0:T(8,128)} %coupling_ref.1) | copy-start | bytes 1732
  14.2 0.7 %copy-start.8 = (s32[8,128]{1,0:T(8,128)S(1)}, s32[8,128]{1,0:T(8,128)}, u32[]{:S(2)}) copy-start(s32[8,128]{1,0:T(8,128)} %light_ref.1) | copy-start | bytes 12292
where the time goes:
time: 59 us; the launch traced here: 58.7 us
  Pallas kernels  54 us (92%)
  local copies, waits for them, and re-layouts  4.62 us (8%)
    pallas_call x1, Pallas kernels, local(): pl.pallas_call(column_kernel, out_shape=jax.ShapeDtypeStruct(tracers.shap...  43.9 us
    pallas_call x1, Pallas kernels, local(): pl.pallas_call(rims, out_shape=(jax.ShapeDtypeStruct((species + 1, rows,...  10.2 us
    unnamed x22, local copies, waits for them, and re-layouts  4.62 us

commit v1 on v0

--- a/solution.py
+++ b/solution.py
@@ -6,7 +6,6 @@
 from jax.sharding import PartitionSpec as P
 
 SUBSTEPS = 16
-CHUNK = 8
 F32 = jnp.float32
 BF16 = jnp.bfloat16
 MESH = pl.DeviceIdType.MESH
@@ -233,7 +232,7 @@
                 ).astype(BF16)
                 out_ref[s, k] = value
                 tile = slice(s * rows, (s + 1) * rows)
-                state[p + 1, tile, lanes] = value.astype(F32)
+                state[p, tile, lanes] = value.astype(F32)
                 rate = table_ref[index_ref[s], k]
                 loss[p, tile, lanes] = jnp.full((rows, cols), rate, F32)
                 base[p, tile, lanes] = jnp.full((rows, cols), 1.0 + rate, F32)
@@ -242,34 +241,29 @@
     lax.fori_loop(0, pairs, advect, 0)
 
     def substep(step, _):
-        def chunk(b, carry):
-            below, flux = carry
-            for i in range(CHUNK):
-                p = b * CHUNK + i
-                q = state[p + 1]
-                high = q.astype(BF16)
-                low = (q - high.astype(F32)).astype(BF16)
-                made = jnp.dot(
-                    matrix[...],
-                    jnp.concatenate([high, low, high, low], axis=0),
-                    preferred_element_type=F32,
-                )
-                under = base[p] + loss[p] * (q * q)
-                guess = pl.reciprocal(under, approx=True)
-                z = (made * guess) * (2.0 - under * guess)
-                for half in range(2):
-                    here = z[:, half * cols : (half + 1) * cols]
-                    k = 2 * p + half
-                    rate = jnp.where(k > 0, kappa_ref[jnp.maximum(k - 1, 0)], 0.0)
-                    upward = rate * (here - below)
+        below = flux = None
+        for p in range(pairs):
+            q = state[p]
+            high = q.astype(BF16)
+            low = (q - high.astype(F32)).astype(BF16)
+            made = jnp.dot(
+                matrix[...],
+                jnp.concatenate([high, low, high, low], axis=0),
+                preferred_element_type=F32,
+            )
+            under = base[p] + loss[p] * (q * q)
+            z = made * pl.reciprocal(under, approx=True)
+            for half in range(2):
+                k = 2 * p + half
+                here = z[:, half * cols : (half + 1) * cols]
+                if k > 0:
+                    upward = kappa_ref[k - 1] * (here - below)
+                    done = below + (upward if k == 1 else upward - flux)
                     lanes = slice((1 - half) * cols, (2 - half) * cols)
-                    state[p + half, :, lanes] = below + (upward - flux)
-                    below, flux = here, upward
-            return below, flux
-
-        zero = jnp.zeros((mix, cols), F32)
-        below, flux = lax.fori_loop(0, pairs // CHUNK, chunk, (zero, zero))
-        state[pairs, :, cols:] = below - flux
+                    state[p + half - 1, :, lanes] = done
+                    flux = upward
+                below = here
+        state[pairs - 1, :, cols:] = below - flux
         return 0
 
     lax.fori_loop(0, SUBSTEPS, substep, 0)
@@ -281,7 +275,7 @@
             k = 2 * p + half
             lanes = slice(half * cols, (half + 1) * cols)
             for s in range(species):
-                done = state[p + 1, s * rows : (s + 1) * rows, lanes]
+                done = state[p, s * rows : (s + 1) * rows, lanes]
                 out_ref[s, k] = jnp.where(lit, done, out_ref[s, k].astype(F32)).astype(BF16)
         return 0
 
@@ -347,7 +341,7 @@
             in_specs=[smem()] * 4 + [vmem()] * 8,
             out_specs=vmem(),
             scratch_shapes=[
-                pltpu.VMEM((pairs + 1, mix, 2 * cols), F32),
+                pltpu.VMEM((pairs, mix, 2 * cols), F32),
                 pltpu.VMEM((pairs, mix, 2 * cols), F32),
                 pltpu.VMEM((pairs, mix, 2 * cols), F32),
                 pltpu.VMEM((mix, 4 * mix), F32),

time: 59 us -> 53.2 us (0.902)
  Pallas kernels: 54 us -> 48.2 us
    pallas_call x1, Pallas kernels: 43.9 us -> 38.1 us  [local(): pl.pallas_call(column_kernel, out_shape=jax.ShapeDtypeStruct(tracers.shap...]
where the time goes in v1:
time: 53.2 us; the launch traced here: 52.9 us
  Pallas kernels  48.2 us (91%)
  local copies, waits for them, and re-layouts  4.62 us (9%)
    pallas_call x1, Pallas kernels, local(): pl.pallas_call(column_kernel, out_shape=jax.ShapeDtypeStruct(tracers.shap...  38.1 us
    pallas_call x1, Pallas kernels, local(): pl.pallas_call(rims, out_shape=(jax.ShapeDtypeStruct((species + 1, rows,...  10.2 us
    unnamed x22, local copies, waits for them, and re-layouts  4.62 us

profile of v1, /device:TPU:0, one launch (start us, length us, event | category | flops | bytes accessed | tf_op | source)
XLA Modules:
  0.0 52.9 jit_solution(14044893586214228882)
XLA Ops:
  0.0 0.0 copy-start
  0.0 1.4 %copy-done = bf16[12,64,8,128]{3,2,1,0:T(8,128)(2,1)S(1)} copy-done((bf16[12,64,8,128]{3,2,1,0:T(8,128)(2,1)S(1)}, bf16[12,64,8,128]{3,2,1,0:T(8,128)(2,1)}, u32[]{:S(2)}) %copy-start) | copy-done | bytes 1572888
  1.4 0.0 copy-start.2
  1.4 0.9 %copy-done.2 = bf16[64,8,128]{2,1,0:T(8,128)(2,1)S(1)} copy-done((bf16[64,8,128]{2,1,0:T(8,128)(2,1)S(1)}, bf16[64,8,128]{2,1,0:T(8,128)(2,1)}, u32[]{:S(2)}) %copy-start.2) | copy-done | bytes 131096
  2.3 0.0 copy-start.4
  2.3 0.9 %copy-done.4 = bf16[64,8,128]{2,1,0:T(8,128)(2,1)S(1)} copy-done((bf16[64,8,128]{2,1,0:T(8,128)(2,1)S(1)}, bf16[64,8,128]{2,1,0:T(8,128)(2,1)}, u32[]{:S(2)}) %copy-start.4) | copy-done | bytes 131096
  3.2 0.0 copy-start.1
  3.2 0.0 copy-start.3
  3.2 0.0 copy-start.5
  3.2 0.0 copy-start.7
  3.2 0.0 copy-start.9
  3.2 0.0 copy-start.10
  3.2 10.2 %rims.1 = (f32[13,8,128]{2,1,0:T(8,128)S(1)}, f32[13,8,128]{2,1,0:T(8,128)S(1)}, bf16[768,128]{1,0:T(8,128)(2,1)S(1)}, bf16[832,128]{1,0:T(8,128)(2,1)S(1)}) custom-call(bf16[12,64,8,128]{3,2,1,0:T(8,128)(2,1)S(1)} %copy-done, bf16[64,8,128]{2,1,0:T(8,128)(2,1)S(1)} %copy-done.2, bf16[64,8,128]{2,1,0:T(8,128)(2,1)S(1)} %copy-done.4), custom_call_target="tpu_custom_call" | custom-call | tf_op jit(solution)/shard_map/rims/pallas_call | solution.py:314
  13.4 0.0 copy-done.1
  13.4 0.0 copy-done.3
  13.4 0.0 copy-done.5
  13.4 0.0 copy-done.7
  13.5 0.0 copy-done.9
  13.5 0.0 copy-done.10
  13.5 0.0 copy-start.6
  13.5 0.7 %copy-done.6 = f32[12,12]{1,0:T(8,128)S(1)} copy-done((f32[12,12]{1,0:T(8,128)S(1)}, f32[12,12]{1,0:T(8,128)}, u32[]{:S(2)}) %copy-start.6) | copy-done | bytes 600
  14.2 0.0 copy-start.8
  14.2 0.7 %copy-done.8 = s32[8,128]{1,0:T(8,128)S(1)} copy-done((s32[8,128]{1,0:T(8,128)S(1)}, s32[8,128]{1,0:T(8,128)}, u32[]{:S(2)}) %copy-start.8) | copy-done | bytes 4120
  14.9 38.1 %columns.1 = bf16[12,64,8,128]{3,2,1,0:T(8,128)(2,1)} custom-call(f32[12,12]{1,0:T(8,128)S(1)} %copy-done.6, f32[8,64]{1,0:T(8,128)S(1)} %copy-done.7, s32[12]{0:T(128)S(1)} %copy-done.9, f32[63]{0:T(128)S(1)} %copy-done.10, bf16[12,64,8,128]{3,2,1,0:T(8,128)(2,1)S(1)} %copy-done.1, bf16[64,8,128]{2,1,0:T(8,128)(2,1)S(1)} %copy-done.3, ...), custom_call_target="tpu_custom_call" | custom-call | tf_op jit(solution)/shard_map/columns/pallas_call | solution.py:338
Async XLA Ops:
  0.0 1.4 %copy-start = (bf16[12,64,8,128]{3,2,1,0:T(8,128)(2,1)S(1)}, bf16[12,64,8,128]{3,2,1,0:T(8,128)(2,1)}, u32[]{:S(2)}) copy-start(bf16[12,64,8,128]{3,2,1,0:T(8,128)(2,1)} %c_ref.1) | copy-start | bytes 4718596
  1.4 0.9 %copy-start.2 = (bf16[64,8,128]{2,1,0:T(8,128)(2,1)S(1)}, bf16[64,8,128]{2,1,0:T(8,128)(2,1)}, u32[]{:S(2)}) copy-start(bf16[64,8,128]{2,1,0:T(8,128)(2,1)} %u_ref.1) | copy-start | bytes 393220
  2.3 0.9 %copy-start.4 = (bf16[64,8,128]{2,1,0:T(8,128)(2,1)S(1)}, bf16[64,8,128]{2,1,0:T(8,128)(2,1)}, u32[]{:S(2)}) copy-start(bf16[64,8,128]{2,1,0:T(8,128)(2,1)} %v_ref.1) | copy-start | bytes 393220
  3.2 10.2 %copy-start.1 = (bf16[12,64,8,128]{3,2,1,0:T(8,128)(2,1)S(1)}, bf16[12,64,8,128]{3,2,1,0:T(8,128)(2,1)}, u32[]{:S(2)}) copy-start(bf16[12,64,8,128]{3,2,1,0:T(8,128)(2,1)} %c_ref.1) | copy-start | bytes 4718596
  3.2 10.2 %copy-start.3 = (bf16[64,8,128]{2,1,0:T(8,128)(2,1)S(1)}, bf16[64,8,128]{2,1,0:T(8,128)(2,1)}, u32[]{:S(2)}) copy-start(bf16[64,8,128]{2,1,0:T(8,128)(2,1)} %u_ref.1) | copy-start | bytes 393220
  3.2 10.2 %copy-start.5 = (bf16[64,8,128]{2,1,0:T(8,128)(2,1)S(1)}, bf16[64,8,128]{2,1,0:T(8,128)(2,1)}, u32[]{:S(2)}) copy-start(bf16[64,8,128]{2,1,0:T(8,128)(2,1)} %v_ref.1) | copy-start | bytes 393220
  3.2 10.2 %copy-start.7 = (f32[8,64]{1,0:T(8,128)S(1)}, f32[8,64]{1,0:T(8,128)}, u32[]{:S(2)}) copy-start(f32[8,64]{1,0:T(8,128)} %table_ref.1) | copy-start | bytes 6148
  3.2 10.2 %copy-start.9 = (s32[12]{0:T(128)S(1)}, s32[12]{0:T(128)}, u32[]{:S(2)}) copy-start(s32[12]{0:T(128)} %index_ref.1) | copy-start | bytes 148
  3.2 10.2 %copy-start.10 = (f32[63]{0:T(128)S(1)}, f32[63]{0:T(128)}, u32[]{:S(2)}) copy-start(f32[63]{0:T(128)} %kappa_ref.1) | copy-start | bytes 760
  13.5 0.7 %copy-start.6 = (f32[12,12]{1,0:T(8,128)S(1)}, f32[12,12]{1,0:T(8,128)}, u32[]{:S(2)}) copy-start(f32[12,12]{1,0:T(8,128)} %coupling_ref.1) | copy-start | bytes 1732
  14.2 0.7 %copy-start.8 = (s32[8,128]{1,0:T(8,128)S(1)}, s32[8,128]{1,0:T(8,128)}, u32[]{:S(2)}) copy-start(s32[8,128]{1,0:T(8,128)} %light_ref.1) | copy-start | bytes 12292
